TPU v7x, 256 devices: a whole 4x4x8 slice. The times are simulated.
256 devices in a mesh: dec: 32 (over y, x, core), ch: 8 (over z).
Axes of the slice: x: 4, y: 4, z: 8, core: 2. Of those that a mesh axis runs over, the one named last changes fastest.
Arguments:
- frame_cotangent: bfloat16 [256, 160, 8192], P('dec', None, 'ch'), may hold values from -5 to 5
- rollout_utterance: int32 [256], P('dec'), may hold values from 0 to 31, as said below
- frame_offset: int32 [256], P('dec'), may hold values from 0 to 32
- utterance_frames: int32 [32], P('dec'), may hold values from 1 to 128, 3072 in all
- normed_input: bfloat16 [32, 128, 1024], P('dec', None, 'ch'), may hold values from -6 to 6
- expand_weight: bfloat16 [1024, 2, 1024], P(None, None, 'ch'), may hold values from -0.1875 to 0.1875
- depth_kernel: bfloat16 [9, 1024], P(None, 'ch'), may hold values from -2 to 2
- norm_scale: float32 [1024], P('ch'), may hold values from 0.1 to 1.9
- norm_shift: float32 [1024], P('ch'), may hold values from -3 to 3
- project_weight: bfloat16 [1024, 1024], replicated, may hold values from -0.1875 to 0.1875
- adapter_weight: bfloat16 [1024, 8192], P(None, 'ch'), may hold values from -0.0625 to 0.0625
Outputs:
- grad_stream: bfloat16 [32, 128, 1024], P('dec', None, 'ch')
- grad_normed: bfloat16 [32, 128, 1024], P('dec', None, 'ch')
Inputs may be any that keep to these rules, and one draw needn't show every extreme that they name: `rollout_utterance`: each utterance is named by exactly 8 rollouts; utterances k * 1 to (k + 1) - 1 are owned by index k of dec; among the 8 rollouts of one index of dec at most 1 name utterances of one owner, and some owner is named exactly 1 times; the rollouts of index k of dec always name some utterance of the owner (k + 16) mod 32.
All inputs are finite; a program needn't handle non-finite values. No bound on the sum of `utterance_frames` on one device may be relied on, other than what follows from the above.
Results may differ from a plain program's by a relative error of at most 0.03.
Values may be sent and summed in bfloat16 or wider, within the bound.
A program may use at most 128 MiB of HBM per device.

v0:
```python
import jax
import jax.numpy as jnp
from jax import lax
from jax.sharding import PartitionSpec as P


def body(
    frame_cotangent,
    rollout_utterance,
    frame_offset,
    utterance_frames,
    normed_input,
    expand_weight,
    depth_kernel,
    norm_scale,
    norm_shift,
    project_weight,
    adapter_weight,
):
    local_rolls, seq_len, d_local = frame_cotangent.shape
    u_local, frames, c_local = normed_input.shape
    width = expand_weight.shape[0]
    taps = depth_kernel.shape[0]
    row_count = u_local * frames
    slabs = jax.vmap(lambda window, first: lax.dynamic_slice_in_dim(window, first, frames, 0))(
        frame_cotangent, frame_offset
    )
    flat_slabs = slabs.reshape(local_rolls, frames * d_local)
    target = jnp.arange(lax.axis_size("dec") * u_local, dtype=jnp.int32)
    select = (target[:, None] == rollout_utterance[None, :]).astype(jnp.bfloat16)
    rounded = lax.optimization_barrier(
        jnp.dot(select, flat_slabs, preferred_element_type=jnp.float32).astype(jnp.bfloat16)
    )
    received = lax.psum_scatter(
        rounded.astype(jnp.float32).astype(jnp.bfloat16), "dec", scatter_dimension=0, tiled=True
    ).astype(jnp.float32)
    frame_index = jnp.arange(frames, dtype=jnp.int32)
    mask = (frame_index[None, :] < utterance_frames[:, None]).astype(jnp.float32)
    frame_grad = (received.reshape(u_local, frames, d_local) * mask[:, :, None]).astype(
        jnp.bfloat16
    )
    grad_rows = frame_grad.reshape(row_count, d_local)
    block = adapter_weight
    stream_cols = lax.psum_scatter(
        lax.dot_general(
            block, grad_rows, (((1,), (1,)), ((), ())), preferred_element_type=jnp.float32
        ).astype(jnp.bfloat16),
        "ch",
        scatter_dimension=0,
        tiled=True,
    ).astype(jnp.float32)
    grad_stream = stream_cols.T.astype(jnp.bfloat16)
    expand_flat = expand_weight.reshape(width, 2 * c_local)
    piece = lax.all_gather(normed_input, "ch", axis=2, tiled=True)
    span = piece.shape[2]
    block = expand_flat
    expanded = jnp.dot(piece.reshape(row_count, span), block, preferred_element_type=jnp.float32)
    value = expanded[:, :c_local]
    gate = expanded[:, c_local:]
    sig_gate = jax.nn.sigmoid(gate)
    mask_rows = mask.reshape(row_count, 1)
    glu = (mask_rows * value * sig_gate).reshape(u_local, frames, c_local)
    kernel = depth_kernel.astype(jnp.float32)
    half = (taps - 1) // 2
    padded = jnp.pad(glu, ((0, 0), (half, half), (0, 0)))
    depth = jnp.zeros((u_local, frames, c_local), jnp.float32)
    for step in range(taps):
        depth = depth + kernel[step] * padded[:, step : step + frames, :]
    shifted = depth * norm_scale + norm_shift
    ch_start = lax.axis_index("ch") * c_local
    own_rows = lax.dynamic_slice_in_dim(project_weight, ch_start, c_local, 0)
    grad_swish = lax.dot_general(
        lax.all_gather(grad_stream, "ch", axis=1, tiled=True),
        own_rows,
        (((1,), (1,)), ((), ())),
        preferred_element_type=jnp.float32,
    )
    grad_swish = grad_swish.reshape(u_local, frames, c_local)
    sig_shift = jax.nn.sigmoid(shifted)
    grad_depth = grad_swish * sig_shift * (1.0 + shifted * (1.0 - sig_shift)) * norm_scale
    padded_back = jnp.pad(grad_depth, ((0, 0), (half, half), (0, 0)))
    grad_glu = jnp.zeros((u_local, frames, c_local), jnp.float32)
    for step in range(taps):
        grad_glu = (
            grad_glu + kernel[step] * padded_back[:, taps - 1 - step : taps - 1 - step + frames, :]
        )
    grad_glu = grad_glu.reshape(row_count, c_local) * mask_rows
    grad_value = grad_glu * sig_gate
    grad_gate = grad_glu * value * sig_gate * (1.0 - sig_gate)
    grad_expanded = jnp.concatenate([grad_value, grad_gate], axis=1).astype(jnp.bfloat16)
    block = expand_flat
    input_cols = lax.psum_scatter(
        lax.dot_general(
            block, grad_expanded, (((1,), (1,)), ((), ())), preferred_element_type=jnp.float32
        ).astype(jnp.bfloat16),
        "ch",
        scatter_dimension=0,
        tiled=True,
    ).astype(jnp.float32)
    grad_normed = input_cols.T.astype(jnp.bfloat16)
    return (
        grad_stream.reshape(u_local, frames, c_local),
        grad_normed.reshape(u_local, frames, c_local),
    )


def solution(mesh):
    return jax.shard_map(
        body,
        mesh=mesh,
        in_specs=(
            P("dec", None, "ch"),
            P("dec"),
            P("dec"),
            P("dec"),
            P("dec", None, "ch"),
            P(None, None, "ch"),
            P(None, "ch"),
            P("ch"),
            P("ch"),
            P(),
            P(None, "ch"),
        ),
        out_specs=(P("dec", None, "ch"), P("dec", None, "ch")),
        check_vma=False,
    )
```

profile of v0, /device:TPU:2, one launch (start us, length us, event | category | flops | bytes accessed | tf_op | source)
XLA Modules:
  0.0 291.1 jit_solution(7985115832883132730)
XLA Ops:
  7.2 0.8 fusion.34
  8.0 29.7 %while.1 = (s32[]{:T(128)}, bf16[8,160,1024]{2,1,0:T(8,128)(2,1)}, s32[8,3]{0,1:T(4,128)S(1)}, bf16[8,128,1024]{2,1,0:T(8,128)(2,1)}, s32[]{:T(128)}) while((s32[]{:T(128)}, bf16[8,160,1024]{2,1,0:T(8,128)(2,1)}, s32[8,3]{0,1:T(4,128)S(1)}, bf16[8,128,1024]{2,1,0:T(8,128)(2,1)}, s32[]{:T(128)}) %tuple.32), condition=%wide.while_cond, body=%wide.while_body.sunk | while | flops 2 | bytes 525429 | solution.py:25
  8.1 0.1 constant_dynamic-slice_fusion.2
  8.1 0.6 fusion.42
  8.7 3.1 %dynamic-slice_dynamic-update-slice_fusion.2 = bf16[8,128,1024]{2,1,0:T(8,128)(2,1)} fusion(bf16[8,128,1024]{2,1,0:T(8,128)(2,1)} %get-tuple-element.68, s32[]{:T(128)S(6)} %copy.30, bf16[8,160,1024]{2,1,0:T(8,128)(2,1)} %get-tuple-element.71, s32[]{:T(128)} %bitcast.81, s32[]{:T(128)} %bitcast.82), kind=kLoop, calls=%fused_computation.clone.1 | loop fusion | bytes 525316 | tf_op jit(solution)/shard_map/vmap()/gather
  11.8 0.1 constant_dynamic-slice_fusion.2
  11.8 0.6 fusion.42
  12.4 3.1 %dynamic-slice_dynamic-update-slice_fusion.2 = bf16[8,128,1024]{2,1,0:T(8,128)(2,1)} fusion(bf16[8,128,1024]{2,1,0:T(8,128)(2,1)} %get-tuple-element.68, s32[]{:T(128)S(6)} %copy.30, bf16[8,160,1024]{2,1,0:T(8,128)(2,1)} %get-tuple-element.71, s32[]{:T(128)} %bitcast.81, s32[]{:T(128)} %bitcast.82), kind=kLoop, calls=%fused_computation.clone.1 | loop fusion | bytes 525316 | tf_op jit(solution)/shard_map/vmap()/gather
  15.5 0.1 constant_dynamic-slice_fusion.2
  15.6 0.6 fusion.42
  16.1 3.0 %dynamic-slice_dynamic-update-slice_fusion.2 = bf16[8,128,1024]{2,1,0:T(8,128)(2,1)} fusion(bf16[8,128,1024]{2,1,0:T(8,128)(2,1)} %get-tuple-element.68, s32[]{:T(128)S(6)} %copy.30, bf16[8,160,1024]{2,1,0:T(8,128)(2,1)} %get-tuple-element.71, s32[]{:T(128)} %bitcast.81, s32[]{:T(128)} %bitcast.82), kind=kLoop, calls=%fused_computation.clone.1 | loop fusion | bytes 525316 | tf_op jit(solution)/shard_map/vmap()/gather
  19.2 0.1 constant_dynamic-slice_fusion.2
  19.3 0.6 fusion.42
  19.8 3.0 %dynamic-slice_dynamic-update-slice_fusion.2 = bf16[8,128,1024]{2,1,0:T(8,128)(2,1)} fusion(bf16[8,128,1024]{2,1,0:T(8,128)(2,1)} %get-tuple-element.68, s32[]{:T(128)S(6)} %copy.30, bf16[8,160,1024]{2,1,0:T(8,128)(2,1)} %get-tuple-element.71, s32[]{:T(128)} %bitcast.81, s32[]{:T(128)} %bitcast.82), kind=kLoop, calls=%fused_computation.clone.1 | loop fusion | bytes 525316 | tf_op jit(solution)/shard_map/vmap()/gather
  22.9 0.1 constant_dynamic-slice_fusion.2
  22.9 0.6 fusion.42
  23.5 3.1 %dynamic-slice_dynamic-update-slice_fusion.2 = bf16[8,128,1024]{2,1,0:T(8,128)(2,1)} fusion(bf16[8,128,1024]{2,1,0:T(8,128)(2,1)} %get-tuple-element.68, s32[]{:T(128)S(6)} %copy.30, bf16[8,160,1024]{2,1,0:T(8,128)(2,1)} %get-tuple-element.71, s32[]{:T(128)} %bitcast.81, s32[]{:T(128)} %bitcast.82), kind=kLoop, calls=%fused_computation.clone.1 | loop fusion | bytes 525316 | tf_op jit(solution)/shard_map/vmap()/gather
  26.6 0.1 constant_dynamic-slice_fusion.2
  26.7 0.6 fusion.42
  27.2 3.1 %dynamic-slice_dynamic-update-slice_fusion.2 = bf16[8,128,1024]{2,1,0:T(8,128)(2,1)} fusion(bf16[8,128,1024]{2,1,0:T(8,128)(2,1)} %get-tuple-element.68, s32[]{:T(128)S(6)} %copy.30, bf16[8,160,1024]{2,1,0:T(8,128)(2,1)} %get-tuple-element.71, s32[]{:T(128)} %bitcast.81, s32[]{:T(128)} %bitcast.82), kind=kLoop, calls=%fused_computation.clone.1 | loop fusion | bytes 525316 | tf_op jit(solution)/shard_map/vmap()/gather
  30.3 0.1 constant_dynamic-slice_fusion.2
  30.4 0.6 fusion.42
  31.0 3.1 %dynamic-slice_dynamic-update-slice_fusion.2 = bf16[8,128,1024]{2,1,0:T(8,128)(2,1)} fusion(bf16[8,128,1024]{2,1,0:T(8,128)(2,1)} %get-tuple-element.68, s32[]{:T(128)S(6)} %copy.30, bf16[8,160,1024]{2,1,0:T(8,128)(2,1)} %get-tuple-element.71, s32[]{:T(128)} %bitcast.81, s32[]{:T(128)} %bitcast.82), kind=kLoop, calls=%fused_computation.clone.1 | loop fusion | bytes 525316 | tf_op jit(solution)/shard_map/vmap()/gather
  34.0 0.1 constant_dynamic-slice_fusion.2
  34.1 0.6 fusion.42
  34.7 3.1 %dynamic-slice_dynamic-update-slice_fusion.2 = bf16[8,128,1024]{2,1,0:T(8,128)(2,1)} fusion(bf16[8,128,1024]{2,1,0:T(8,128)(2,1)} %get-tuple-element.68, s32[]{:T(128)S(6)} %copy.30, bf16[8,160,1024]{2,1,0:T(8,128)(2,1)} %get-tuple-element.71, s32[]{:T(128)} %bitcast.81, s32[]{:T(128)} %bitcast.82), kind=kLoop, calls=%fused_computation.clone.1 | loop fusion | bytes 525316 | tf_op jit(solution)/shard_map/vmap()/gather
  37.7 2.8 copy.17
  40.5 5.5 %convolution_convert_fusion = bf16[32,131072]{1,0:T(8,128)(2,1)} fusion(bf16[8,131072]{1,0:T(8,128)(2,1)S(1)} %bitcast.84, s32[8]{0:T(128)S(1)} %copy-done.5), kind=kOutput, calls=%fused_computation.2 | convolution fusion | flops 71303424 | bytes 10485792 | tf_op jit(solution)/shard_map/dot_general | solution.py:32
  46.1 0.0 reduce-scatter.7.cloned.1.call-start
  46.8 0.6 dynamic-slice.4
  47.4 132.1 %all-reduce.6.cloned.1.call-done = bf16[32,131072]{1,0:T(8,128)(2,1)} async-done(((bf16[32,131072]{1,0:T(8,128)(2,1)}), bf16[32,131072]{1,0:T(8,128)(2,1)}) %all-reduce.6.cloned.1.call-update) | async-done | bytes 8388624
  179.5 3.8 %fusion.8 = f32[131072]{0:T(1024)S(1)} fusion(bf16[32,131072]{1,0:T(8,128)(2,1)} %all-reduce.6.cloned.1.call-done, u32[]{:T(128)} %bitcast.26), kind=kLoop, calls=%fused_computation.15 | loop fusion | flops 131072 | bytes 786436 | tf_op jit(solution)/shard_map/reshape | solution.py:39
  183.3 0.1 reshape.134
  183.5 0.8 fusion
  184.3 0.9 copy.13
  185.2 0.0 reduce-scatter.9.cloned.1.call-start
  185.3 24.9 %all_gather.7 = bf16[1,128,1024]{2,1,0:T(8,128)(2,1)S(1)} all-gather(bf16[1,128,128]{2,1,0:T(8,128)(2,1)S(1)} %copy-done.3), channel_id=1, replica_groups=mesh['dec'=32,'ch'=8] {'ch'}, dimensions={2}, use_global_device_ids=true | all-gather | bytes 294912 | tf_op jit(solution)/shard_map/all_gather | solution.py:54
  210.2 0.2 fusion.6
  210.4 0.1 fusion.33
  210.5 11.6 %reduce-scatter.7.cloned.1.call-done = bf16[128,128]{1,0:T(8,128)(2,1)} async-done(((bf16[1024,128]{1,0:T(8,128)(2,1)}), bf16[128,128]{1,0:T(8,128)(2,1)}) %reduce-scatter.7.cloned.1.call-update) | async-done | bytes 32784
  222.1 0.9 copy.14
  223.0 22.2 %all_gather.6 = bf16[128,1024]{1,0:T(8,128)(2,1)S(1)} all-gather(bf16[128,128]{1,0:T(8,128)(2,1)S(1)} %bitcast.88), channel_id=1, replica_groups=mesh['dec'=32,'ch'=8] {'ch'}, dimensions={1}, use_global_device_ids=true | all-gather | bytes 294912 | tf_op jit(solution)/shard_map/all_gather | solution.py:73
  245.2 1.2 fusion.4
  246.4 0.1 multiply_convert_fusion.3
  246.5 0.3 fusion.1
  246.8 0.9 copy.15
  247.7 35.4 %reduce-scatter.9.cloned.1.call-done = bf16[128,128]{1,0:T(8,128)(2,1)} async-done(((bf16[1024,128]{1,0:T(8,128)(2,1)}), bf16[128,128]{1,0:T(8,128)(2,1)}) %reduce-scatter.9.cloned.1.call-update) | async-done | bytes 32784
  283.1 1.5 copy.16
  (29 shorter events, 0.2 us)
Async XLA Ops:
  7.2 176.3 %copy-start = (bf16[1024,1024]{1,0:T(8,128)(2,1)S(1)}, bf16[1024,1024]{1,0:T(8,128)(2,1)}, u32[]{:S(2)}) copy-start(bf16[1024,1024]{1,0:T(8,128)(2,1)} %param.21) | copy-start | bytes 6291460
  7.2 172.3 %all-reduce.6.cloned.1.call-start = ((), (), s32[]{:S(2)}) async-start(), calls=%async_computation.4 | async-start | bytes 16777216
  37.7 2.8 copy-start.5
  46.0 0.7 copy-start.4
  46.1 0.8 copy-start.8
  46.1 176.0 %reduce-scatter.7.cloned.1.call-start = ((), (), s32[]{:S(2)}) async-start(), calls=%async_computation.2 | async-start | bytes 294912
  183.4 1.8 copy-start.3
  183.5 26.7 %copy-start.1 = (bf16[1024,2,128]{2,1,0:T(2,128)(2,1)S(1)}, bf16[1024,2,128]{2,1,0:T(2,128)(2,1)}, u32[]{:S(2)}) copy-start(bf16[1024,2,128]{2,1,0:T(2,128)(2,1)} %param.16) | copy-start | bytes 1572868
  183.5 61.7 %copy-start.6 = (f32[128]{0:T(128)S(1)}, f32[128]{0:T(128)}, u32[]{:S(2)}) copy-start(f32[128]{0:T(128)} %param.19) | copy-start | bytes 1540
  183.5 61.7 %copy-start.7 = (f32[128]{0:T(128)S(1)}, f32[128]{0:T(128)}, u32[]{:S(2)}) copy-start(f32[128]{0:T(128)} %param.18) | copy-start | bytes 1540
  185.2 97.9 %reduce-scatter.9.cloned.1.call-start = ((), (), s32[]{:S(2)}) async-start(), calls=%async_computation.3 | async-start | bytes 294912
  223.0 61.6 %copy-start.2 = (bf16[128,128]{0,1:T(8,128)(2,1)}, bf16[128,128]{0,1:T(8,128)(2,1)S(1)}, u32[]{:S(2)}) copy-start(bf16[128,128]{0,1:T(8,128)(2,1)S(1)} %copy.14) | copy-start | bytes 98308
Sparse Core Ops, SparseCore 0:
  46.2 133.2 all-reduce.5
  185.3 36.7 reduce-scatter.6
  247.8 35.2 reduce-scatter.8
where the time goes:
time: 292 us; the launch traced here: 291 us
  waiting for transfers between devices  179 us (61%)
  blocking collectives  47.1 us (16%)
  local copies, waits for them, and re-layouts  37.2 us (13%)
  between operations  14.6 us (5%)
  matrix products  8.12 us (3%)
  other arithmetic  4.86 us (2%)
    unnamed x6, waiting for transfers between devices  179 us
    gather x24, local copies, waits for them, and re-layouts  29.7 us
    all_gather x1, blocking collectives, body(): piece = lax.all_gather(normed_input, 'ch', axis=2, tiled=True)  24.9 us
    all_gather x1, blocking collectives, body(): lax.all_gather(grad_stream, 'ch', axis=1, tiled=True)  22.2 us
    unnamed x25, local copies, waits for them, and re-layouts  7.43 us
  transfers between devices with their start and end apart: 3, of which 3 were waited for; matrix products, arithmetic and copies ran while one was open for 0% of the time, Pallas kernels for 0%

commit v1 on v0

--- a/solution.py
+++ b/solution.py
@@ -70,7 +70,9 @@
     ch_start = lax.axis_index("ch") * c_local
     own_rows = lax.dynamic_slice_in_dim(project_weight, ch_start, c_local, 0)
     grad_swish = lax.dot_general(
-        lax.all_gather(grad_stream, "ch", axis=1, tiled=True),
+        jnp.concatenate(
+            lax.all_to_all(jnp.stack([grad_stream] * lax.axis_size("ch")), "ch", 0, 0), axis=1
+        ),
         own_rows,
         (((1,), (1,)), ((), ())),
         preferred_element_type=jnp.float32,

time: 292 us -> 281 us (0.962)
  blocking collectives: 47.1 us -> 24.8 us
  waiting for transfers between devices: 179 us -> 187 us
  starting transfers between devices: 0.12 us -> 4.55 us
    all_gather x1 -> x0, blocking collectives: 22.2 us -> none  [body(): lax.all_gather(grad_stream, 'ch', axis=1, tiled=True)]
    all_to_all x0 -> x1, waiting for transfers between devices: none -> 10 us  [body(): lax.all_to_all(jnp.stack([grad_stream] * lax.axis_size('ch')), 'ch', 0, 0)]
    all_to_all x0 -> x1, starting transfers between devices: none -> 4.43 us  [body(): lax.all_to_all(jnp.stack([grad_stream] * lax.axis_size('ch')), 'ch', 0, 0)]
  transfers between devices with their start and end apart: 3 -> 4, of which waited for: 3 -> 4; matrix products, arithmetic and copies ran while one was open for 0% -> 1% of each run, Pallas kernels for 0% -> 0%
where the time goes in v1:
time: 281 us
  waiting for transfers between devices  187 us (67%)
  local copies, waits for them, and re-layouts  37.1 us (13%)
  blocking collectives  24.8 us (9%)
  between operations  14.6 us (5%)
  matrix products  8.14 us (3%)
  other arithmetic  4.86 us (2%)
  starting transfers between devices  4.55 us (2%)
    unnamed x6, waiting for transfers between devices  177 us
    gather x24, local copies, waits for them, and re-layouts  28.2 us
    all_gather x1, blocking collectives, body(): piece = lax.all_gather(normed_input, 'ch', axis=2, tiled=True)  24.8 us
    all_to_all x1, waiting for transfers between devices, body(): lax.all_to_all(jnp.stack([grad_stream] * lax.axis_size('ch')), 'ch', 0, 0)  10 us
    unnamed x25, local copies, waits for them, and re-layouts  7.28 us
  transfers between devices with their start and end apart: 4, of which 4 were waited for; matrix products, arithmetic and copies ran while one was open for 1% of the time, Pallas kernels for 0%

profile of v1, /device:TPU:2, one launch (start us, length us, event | category | flops | bytes accessed | tf_op | source)
XLA Modules:
  0.0 280.6 jit_solution(7788294665481093370)
XLA Ops:
  7.2 0.8 fusion.34
  8.0 28.3 %while.1 = (s32[]{:T(128)}, bf16[8,160,1024]{2,1,0:T(8,128)(2,1)}, s32[8,3]{0,1:T(4,128)S(1)}, bf16[8,128,1024]{2,1,0:T(8,128)(2,1)}, s32[]{:T(128)}) while((s32[]{:T(128)}, bf16[8,160,1024]{2,1,0:T(8,128)(2,1)}, s32[8,3]{0,1:T(4,128)S(1)}, bf16[8,128,1024]{2,1,0:T(8,128)(2,1)}, s32[]{:T(128)}) %tuple.32), condition=%wide.while_cond, body=%wide.while_body.sunk | while | flops 2 | bytes 525429 | solution.py:25
  8.1 0.1 constant_dynamic-slice_fusion.2
  8.1 0.5 fusion.42
  8.7 2.9 %dynamic-slice_dynamic-update-slice_fusion.2 = bf16[8,128,1024]{2,1,0:T(8,128)(2,1)} fusion(bf16[8,128,1024]{2,1,0:T(8,128)(2,1)} %get-tuple-element.68, s32[]{:T(128)S(6)} %copy.33, bf16[8,160,1024]{2,1,0:T(8,128)(2,1)} %get-tuple-element.71, s32[]{:T(128)} %bitcast.85, s32[]{:T(128)} %bitcast.86), kind=kLoop, calls=%fused_computation.clone.1 | loop fusion | bytes 525316 | tf_op jit(solution)/shard_map/vmap()/gather
  11.6 0.1 constant_dynamic-slice_fusion.2
  11.7 0.5 fusion.42
  12.2 2.9 %dynamic-slice_dynamic-update-slice_fusion.2 = bf16[8,128,1024]{2,1,0:T(8,128)(2,1)} fusion(bf16[8,128,1024]{2,1,0:T(8,128)(2,1)} %get-tuple-element.68, s32[]{:T(128)S(6)} %copy.33, bf16[8,160,1024]{2,1,0:T(8,128)(2,1)} %get-tuple-element.71, s32[]{:T(128)} %bitcast.85, s32[]{:T(128)} %bitcast.86), kind=kLoop, calls=%fused_computation.clone.1 | loop fusion | bytes 525316 | tf_op jit(solution)/shard_map/vmap()/gather
  15.1 0.1 constant_dynamic-slice_fusion.2
  15.2 0.5 fusion.42
  15.7 2.9 %dynamic-slice_dynamic-update-slice_fusion.2 = bf16[8,128,1024]{2,1,0:T(8,128)(2,1)} fusion(bf16[8,128,1024]{2,1,0:T(8,128)(2,1)} %get-tuple-element.68, s32[]{:T(128)S(6)} %copy.33, bf16[8,160,1024]{2,1,0:T(8,128)(2,1)} %get-tuple-element.71, s32[]{:T(128)} %bitcast.85, s32[]{:T(128)} %bitcast.86), kind=kLoop, calls=%fused_computation.clone.1 | loop fusion | bytes 525316 | tf_op jit(solution)/shard_map/vmap()/gather
  18.6 0.1 constant_dynamic-slice_fusion.2
  18.7 0.5 fusion.42
  19.2 2.9 %dynamic-slice_dynamic-update-slice_fusion.2 = bf16[8,128,1024]{2,1,0:T(8,128)(2,1)} fusion(bf16[8,128,1024]{2,1,0:T(8,128)(2,1)} %get-tuple-element.68, s32[]{:T(128)S(6)} %copy.33, bf16[8,160,1024]{2,1,0:T(8,128)(2,1)} %get-tuple-element.71, s32[]{:T(128)} %bitcast.85, s32[]{:T(128)} %bitcast.86), kind=kLoop, calls=%fused_computation.clone.1 | loop fusion | bytes 525316 | tf_op jit(solution)/shard_map/vmap()/gather
  22.2 0.1 constant_dynamic-slice_fusion.2
  22.2 0.5 fusion.42
  22.8 2.9 %dynamic-slice_dynamic-update-slice_fusion.2 = bf16[8,128,1024]{2,1,0:T(8,128)(2,1)} fusion(bf16[8,128,1024]{2,1,0:T(8,128)(2,1)} %get-tuple-element.68, s32[]{:T(128)S(6)} %copy.33, bf16[8,160,1024]{2,1,0:T(8,128)(2,1)} %get-tuple-element.71, s32[]{:T(128)} %bitcast.85, s32[]{:T(128)} %bitcast.86), kind=kLoop, calls=%fused_computation.clone.1 | loop fusion | bytes 525316 | tf_op jit(solution)/shard_map/vmap()/gather
  25.7 0.1 constant_dynamic-slice_fusion.2
  25.8 0.5 fusion.42
  26.3 2.9 %dynamic-slice_dynamic-update-slice_fusion.2 = bf16[8,128,1024]{2,1,0:T(8,128)(2,1)} fusion(bf16[8,128,1024]{2,1,0:T(8,128)(2,1)} %get-tuple-element.68, s32[]{:T(128)S(6)} %copy.33, bf16[8,160,1024]{2,1,0:T(8,128)(2,1)} %get-tuple-element.71, s32[]{:T(128)} %bitcast.85, s32[]{:T(128)} %bitcast.86), kind=kLoop, calls=%fused_computation.clone.1 | loop fusion | bytes 525316 | tf_op jit(solution)/shard_map/vmap()/gather
  29.2 0.1 constant_dynamic-slice_fusion.2
  29.3 0.5 fusion.42
  29.8 2.9 %dynamic-slice_dynamic-update-slice_fusion.2 = bf16[8,128,1024]{2,1,0:T(8,128)(2,1)} fusion(bf16[8,128,1024]{2,1,0:T(8,128)(2,1)} %get-tuple-element.68, s32[]{:T(128)S(6)} %copy.33, bf16[8,160,1024]{2,1,0:T(8,128)(2,1)} %get-tuple-element.71, s32[]{:T(128)} %bitcast.85, s32[]{:T(128)} %bitcast.86), kind=kLoop, calls=%fused_computation.clone.1 | loop fusion | bytes 525316 | tf_op jit(solution)/shard_map/vmap()/gather
  32.8 0.1 constant_dynamic-slice_fusion.2
  32.8 0.5 fusion.42
  33.3 3.0 %dynamic-slice_dynamic-update-slice_fusion.2 = bf16[8,128,1024]{2,1,0:T(8,128)(2,1)} fusion(bf16[8,128,1024]{2,1,0:T(8,128)(2,1)} %get-tuple-element.68, s32[]{:T(128)S(6)} %copy.33, bf16[8,160,1024]{2,1,0:T(8,128)(2,1)} %get-tuple-element.71, s32[]{:T(128)} %bitcast.85, s32[]{:T(128)} %bitcast.86), kind=kLoop, calls=%fused_computation.clone.1 | loop fusion | bytes 525316 | tf_op jit(solution)/shard_map/vmap()/gather
  36.3 2.8 copy.20
  39.1 5.5 %convolution_convert_fusion = bf16[32,131072]{1,0:T(8,128)(2,1)} fusion(bf16[8,131072]{1,0:T(8,128)(2,1)S(1)} %bitcast.88, s32[8]{0:T(128)S(1)} %copy-done.5), kind=kOutput, calls=%fused_computation.2 | convolution fusion | flops 71303424 | bytes 10485792 | tf_op jit(solution)/shard_map/dot_general | solution.py:32
  45.3 0.6 dynamic-slice.4
  45.9 132.1 %all-reduce.6.cloned.1.call-done = bf16[32,131072]{1,0:T(8,128)(2,1)} async-done(((bf16[32,131072]{1,0:T(8,128)(2,1)}), bf16[32,131072]{1,0:T(8,128)(2,1)}) %all-reduce.6.cloned.1.call-update) | async-done | bytes 8388624
  178.1 3.8 %fusion.8 = f32[131072]{0:T(1024)S(1)} fusion(bf16[32,131072]{1,0:T(8,128)(2,1)} %all-reduce.6.cloned.1.call-done, u32[]{:T(128)} %bitcast.28), kind=kLoop, calls=%fused_computation.15 | loop fusion | flops 131072 | bytes 786436 | tf_op jit(solution)/shard_map/reshape | solution.py:39
  181.9 0.1 reshape.144
  182.0 0.8 fusion
  182.9 0.8 copy.15
  183.8 24.8 %all_gather.3 = bf16[1,128,1024]{2,1,0:T(8,128)(2,1)S(1)} all-gather(bf16[1,128,128]{2,1,0:T(8,128)(2,1)S(1)} %copy-done.3), channel_id=1, replica_groups=mesh['dec'=32,'ch'=8] {'ch'}, dimensions={2}, use_global_device_ids=true | all-gather | bytes 294912 | tf_op jit(solution)/shard_map/all_gather | solution.py:54
  208.6 12.1 %reduce-scatter.7.cloned.1.call-done = bf16[128,128]{1,0:T(8,128)(2,1)} async-done(((bf16[1024,128]{1,0:T(8,128)(2,1)}), bf16[128,128]{1,0:T(8,128)(2,1)}) %reduce-scatter.7.cloned.1.call-update) | async-done | bytes 32784
  220.7 1.5 stack.2
  222.1 4.4 %all-to-all-start = ((bf16[8,128,128]{1,2,0:T(8,128)(2,1)}), bf16[8,128,128]{1,2,0:T(8,128)(2,1)S(1)}, u32[]{:S(2)}, u32[]{:S(2)}) async-start(bf16[8,128,128]{1,2,0:T(8,128)(2,1)} %stack.2), calls=%async_computation | async-start | bytes 524288 | tf_op jit(solution)/shard_map/all_to_all | solution.py:74
  226.6 0.2 fusion.6
  226.9 0.1 fusion.33
  227.0 10.0 %all-to-all-done = bf16[8,128,128]{1,2,0:T(8,128)(2,1)S(1)} async-done(((bf16[8,128,128]{1,2,0:T(8,128)(2,1)}), bf16[8,128,128]{1,2,0:T(8,128)(2,1)S(1)}, u32[]{:S(2)}, u32[]{:S(2)}) %all-to-all-start) | async-done | bytes 262176 | tf_op jit(solution)/shard_map/all_to_all | solution.py:74
  237.1 1.2 fusion.4
  238.3 0.1 multiply_convert_fusion.3
  238.4 0.3 fusion.1
  238.8 0.8 copy.17
  239.6 0.7 copy.16
  240.4 32.3 %reduce-scatter.9.cloned.1.call-done = bf16[128,128]{1,0:T(8,128)(2,1)} async-done(((bf16[1024,128]{1,0:T(8,128)(2,1)}), bf16[128,128]{1,0:T(8,128)(2,1)}) %reduce-scatter.9.cloned.1.call-update) | async-done | bytes 32784
  272.6 1.5 copy.18
  (31 shorter events, 0.3 us)
Async XLA Ops:
  7.2 174.8 %copy-start = (bf16[1024,1024]{1,0:T(8,128)(2,1)S(1)}, bf16[1024,1024]{1,0:T(8,128)(2,1)}, u32[]{:S(2)}) copy-start(bf16[1024,1024]{1,0:T(8,128)(2,1)} %param.21) | copy-start | bytes 6291460
  7.2 170.9 %all-reduce.6.cloned.1.call-start = ((), (), s32[]{:S(2)}) async-start(), calls=%async_computation.5 | async-start | bytes 16777216
  36.3 2.8 copy-start.5
  44.6 0.7 copy-start.8
  44.6 176.0 %reduce-scatter.7.cloned.1.call-start = ((), (), s32[]{:S(2)}) async-start(), calls=%async_computation.3 | async-start | bytes 294912
  182.0 1.8 copy-start.3
  182.0 44.6 %copy-start.1 = (bf16[1024,2,128]{2,1,0:T(2,128)(2,1)S(1)}, bf16[1024,2,128]{2,1,0:T(2,128)(2,1)}, u32[]{:S(2)}) copy-start(bf16[1024,2,128]{2,1,0:T(2,128)(2,1)} %param.16) | copy-start | bytes 1572868
  182.8 44.0 %copy-start.4 = (bf16[9,128]{1,0:T(8,128)(2,1)S(1)}, bf16[9,128]{1,0:T(8,128)(2,1)}, u32[]{:S(2)}) copy-start(bf16[9,128]{1,0:T(8,128)(2,1)} %param.17) | copy-start | bytes 6916
  182.9 54.2 %copy-start.6 = (f32[128]{0:T(128)S(1)}, f32[128]{0:T(128)}, u32[]{:S(2)}) copy-start(f32[128]{0:T(128)} %param.19) | copy-start | bytes 1540
  182.9 54.2 %copy-start.7 = (f32[128]{0:T(128)S(1)}, f32[128]{0:T(128)}, u32[]{:S(2)}) copy-start(f32[128]{0:T(128)} %param.18) | copy-start | bytes 1540
  222.1 14.9 %all-to-all-start = ((bf16[8,128,128]{1,2,0:T(8,128)(2,1)}), bf16[8,128,128]{1,2,0:T(8,128)(2,1)S(1)}, u32[]{:S(2)}, u32[]{:S(2)}) async-start(bf16[8,128,128]{1,2,0:T(8,128)(2,1)} %stack.2), calls=%async_computation | async-start | bytes 524288 | tf_op jit(solution)/shard_map/all_to_all | solution.py:74
  226.6 46.0 %reduce-scatter.9.cloned.1.call-start = ((), (), s32[]{:S(2)}) async-start(), calls=%async_computation.4 | async-start | bytes 294912
  226.9 12.7 %copy-start.2 = (bf16[128,128]{1,0:T(8,128)(2,1)S(1)}, bf16[128,128]{1,0:T(8,128)(2,1)}, u32[]{:S(2)}) copy-start(bf16[128,128]{1,0:T(8,128)(2,1)} %reduce-scatter.7.cloned.1.call-done) | copy-start | bytes 98308
Sparse Core Ops, SparseCore 0:
  44.8 133.2 all-reduce.5
  183.9 36.7 reduce-scatter.6
  239.7 32.8 reduce-scatter.8
